TPU v7x, 32 devices: a whole 2x2x4 slice. The times are simulated.
32 devices in a mesh: slab: 2 (over y), row: 4 (over z), col: 4 (over x, core).
Axes of the slice: x: 2, y: 2, z: 4, core: 2. Of those that a mesh axis runs over, the one named last changes fastest.
Arguments:
- inverse: bfloat16 [2, 8192, 4, 2048], P('slab', 'row', None, 'col'), may hold values from -0.0625 to 0.0625
- sources: bfloat16 [2, 4, 8192, 128], P('slab', None, ('row', 'col')), may hold values from -6 to 6
- coupling: float32 [2, 2, 8192], P('slab', None, ('row', 'col')), may hold values from -1 to 1
- plan: int32 [6, 2, 2], replicated, may hold values from 0 to 3
Outputs:
- up_out: bfloat16 [2, 8192, 128], P('slab', ('row', 'col'))
- down_out: bfloat16 [2, 8192, 128], P('slab', ('row', 'col'))
Inputs may be any that keep to these rules, and one draw needn't show every extreme that they name: `plan`: each entry names one of the 4 stored batches of its slab.
All inputs are finite; a program needn't handle non-finite values.
Results may differ from a plain program's by a relative error of at most 0.023.
Values may be sent and summed in bfloat16 or wider, within the bound.
A program may use at most 64 MiB of HBM per device.

v0:
```python
import jax
import jax.numpy as jnp
from jax import lax
from jax.sharding import PartitionSpec as P

TICKS = 6


def shifted(value, axis, steps):
    count = lax.axis_size(axis)
    leading, last = (max(0, -steps), min(count, count - steps))
    return lax.ppermute(value, axis, [(source, source + steps) for source in range(leading, last)])


def per_device(inverse, sources, coupling, plan):
    local_block = inverse[0]
    rows_here = local_block.shape[0]
    matrix = local_block.reshape(rows_here, -1)
    piece_rows = sources.shape[2]
    batch_width = sources.shape[3]
    slab_index = lax.axis_index("slab")
    up_gain = coupling[0, 0][:, None]
    down_gain = coupling[0, 1][:, None]
    stored = sources[0]
    up_out = jnp.zeros((piece_rows, batch_width), jnp.bfloat16)
    down_out = jnp.zeros((piece_rows, batch_width), jnp.bfloat16)
    for tick_index in range(TICKS):
        if tick_index == 0:
            up_recv = up_out
            down_recv = down_out
        else:
            up_recv = shifted(up_out, "slab", 1)
            down_recv = shifted(down_out, "slab", -1)
        up_choice = plan[tick_index, slab_index, 0]
        down_choice = plan[tick_index, slab_index, 1]
        up_source = lax.dynamic_index_in_dim(stored, up_choice, 0, keepdims=False)
        down_source = lax.dynamic_index_in_dim(stored, down_choice, 0, keepdims=False)
        up_in = (up_source.astype(jnp.float32) + up_gain * up_recv.astype(jnp.float32)).astype(
            jnp.bfloat16
        )
        down_in = (
            down_source.astype(jnp.float32) + down_gain * down_recv.astype(jnp.float32)
        ).astype(jnp.bfloat16)
        forward_partial_value = jnp.dot(
            matrix,
            lax.all_gather(up_in, "row", axis=0, tiled=True),
            preferred_element_type=jnp.float32,
        )
        forward_summed = lax.psum_scatter(
            forward_partial_value.astype(jnp.bfloat16), "col", scatter_dimension=0, tiled=True
        )
        up_out = forward_summed
        partial_value = lax.dot_general(
            matrix,
            lax.all_gather(down_in, "col", axis=0, tiled=True),
            (((0,), (0,)), ((), ())),
            preferred_element_type=jnp.float32,
        )
        summed = lax.psum_scatter(
            partial_value.astype(jnp.bfloat16), "row", scatter_dimension=0, tiled=True
        )
        down_out = summed
    return (up_out[None], down_out[None])


def solution(mesh):
    placed = (
        P("slab", "row", None, "col"),
        P("slab", None, ("row", "col"), None),
        P("slab", None, ("row", "col")),
        P(),
    )
    return jax.shard_map(
        per_device,
        mesh=mesh,
        in_specs=placed,
        out_specs=(P("slab", ("row", "col"), None), P("slab", ("row", "col"), None)),
        check_vma=False,
    )
```

profile of v0, /device:TPU:0, one launch (start us, length us, event | category | flops | bytes accessed | tf_op | source)
XLA Modules:
  0.0 548.5 jit_solution(9365157634703068367)
XLA Ops:
  12.7 8.6 %all_gather.42 = bf16[2048,128]{1,0:T(8,128)(2,1)S(1)} all-gather(bf16[512,128]{1,0:T(8,128)(2,1)S(1)} %fusion.12), channel_id=1, replica_groups=mesh['slab'=2,'row'=4,'col'=4] {'col'}, dimensions={0}, use_global_device_ids=true | all-gather | bytes 655360 | tf_op jit(solution)/shard_map/all_gather | solution.py:55
  21.4 10.2 %copy.8 = bf16[256,8,4,512]{3,1,2,0:T(8,128)(2,1)} copy(bf16[256,8,4,512]{3,2,1,0:T(4,128)(2,1)} %bitcast.115) | data formatting | bytes 16777216
  31.6 7.6 %fusion.1 = bf16[2048,128]{1,0:T(8,128)(2,1)} fusion(bf16[2048,128]{1,0:T(8,128)(2,1)S(1)} %all_gather.42, bf16[2048,2048]{1,0:T(8,128)(2,1)} %bitcast.103), kind=kOutput, calls=%fused_computation.13 | convolution fusion | flops 1074003968 | bytes 9437184 | tf_op jit(solution)/shard_map/dot_general | solution.py:53
  39.3 22.6 %reduce-scatter.25.cloned.1.call-done = bf16[512,128]{1,0:T(8,128)(2,1)} async-done(((bf16[2048,128]{1,0:T(8,128)(2,1)}), bf16[512,128]{1,0:T(8,128)(2,1)}) %reduce-scatter.25.cloned.1.call-update) | async-done | bytes 131088 | tf_op jit(solution)/shard_map/reduce_scatter | solution.py:59
  76.2 7.6 %fusion.2 = bf16[2048,128]{1,0:T(8,128)(2,1)} fusion(bf16[2048,128]{1,0:T(8,128)(2,1)S(1)} %all_gather.43, bf16[2048,2048]{1,0:T(8,128)(2,1)} %bitcast.104), kind=kOutput, calls=%fused_computation.14 | convolution fusion | flops 1074003968 | bytes 9437184 | tf_op jit(solution)/shard_map/dot_general | solution.py:53
  83.9 18.5 %reduce-scatter.27.cloned.1.call-done = bf16[512,128]{1,0:T(8,128)(2,1)} async-done(((bf16[2048,128]{1,0:T(8,128)(2,1)}), bf16[512,128]{1,0:T(8,128)(2,1)}) %reduce-scatter.27.cloned.1.call-update) | async-done | bytes 131088 | tf_op jit(solution)/shard_map/reduce_scatter | solution.py:59
  116.7 7.6 %fusion.3 = bf16[2048,128]{1,0:T(8,128)(2,1)} fusion(bf16[2048,128]{1,0:T(8,128)(2,1)S(1)} %all_gather.44, bf16[2048,2048]{1,0:T(8,128)(2,1)} %bitcast.105), kind=kOutput, calls=%fused_computation.15 | convolution fusion | flops 1074003968 | bytes 9437184 | tf_op jit(solution)/shard_map/dot_general | solution.py:53
  124.4 18.5 %reduce-scatter.29.cloned.1.call-done = bf16[512,128]{1,0:T(8,128)(2,1)} async-done(((bf16[2048,128]{1,0:T(8,128)(2,1)}), bf16[512,128]{1,0:T(8,128)(2,1)}) %reduce-scatter.29.cloned.1.call-update) | async-done | bytes 131088 | tf_op jit(solution)/shard_map/reduce_scatter | solution.py:59
  157.2 7.6 %fusion.4 = bf16[2048,128]{1,0:T(8,128)(2,1)} fusion(bf16[2048,128]{1,0:T(8,128)(2,1)S(1)} %all_gather.45, bf16[2048,2048]{1,0:T(8,128)(2,1)} %bitcast.106), kind=kOutput, calls=%fused_computation.16 | convolution fusion | flops 1074003968 | bytes 9437184 | tf_op jit(solution)/shard_map/dot_general | solution.py:53
  164.8 18.5 %reduce-scatter.31.cloned.1.call-done = bf16[512,128]{1,0:T(8,128)(2,1)} async-done(((bf16[2048,128]{1,0:T(8,128)(2,1)}), bf16[512,128]{1,0:T(8,128)(2,1)}) %reduce-scatter.31.cloned.1.call-update) | async-done | bytes 131088 | tf_op jit(solution)/shard_map/reduce_scatter | solution.py:59
  197.7 7.6 %fusion.5 = bf16[2048,128]{1,0:T(8,128)(2,1)} fusion(bf16[2048,128]{1,0:T(8,128)(2,1)S(1)} %all_gather.46, bf16[2048,2048]{1,0:T(8,128)(2,1)} %bitcast.107), kind=kOutput, calls=%fused_computation.17 | convolution fusion | flops 1074003968 | bytes 9437184 | tf_op jit(solution)/shard_map/dot_general | solution.py:53
  209.2 14.7 %reduce-scatter.33.cloned.1.call-done = bf16[512,128]{1,0:T(8,128)(2,1)} async-done(((bf16[2048,128]{1,0:T(8,128)(2,1)}), bf16[512,128]{1,0:T(8,128)(2,1)}) %reduce-scatter.33.cloned.1.call-update) | async-done | bytes 131088 | tf_op jit(solution)/shard_map/reduce_scatter | solution.py:59
  231.2 14.9 %all_gather.36 = bf16[2048,128]{1,0:T(8,128)(2,1)S(1)} all-gather(bf16[512,128]{1,0:T(8,128)(2,1)S(1)} %get-tuple-element.5), channel_id=1, replica_groups=mesh['slab'=2,'row'=4,'col'=4] {'row'}, dimensions={0}, use_global_device_ids=true | all-gather | bytes 655360 | tf_op jit(solution)/shard_map/all_gather | solution.py:46
  252.7 20.2 %reduce-scatter.13.cloned.1.call-done = bf16[512,128]{1,0:T(8,128)(2,1)} async-done(((bf16[2048,128]{1,0:T(8,128)(2,1)}), bf16[512,128]{1,0:T(8,128)(2,1)}) %reduce-scatter.13.cloned.1.call-update) | async-done | bytes 131088 | tf_op jit(solution)/shard_map/reduce_scatter | solution.py:49
  279.5 14.8 %all_gather.37 = bf16[2048,128]{1,0:T(8,128)(2,1)S(1)} all-gather(bf16[512,128]{1,0:T(8,128)(2,1)S(1)} %fusion.19), channel_id=1, replica_groups=mesh['slab'=2,'row'=4,'col'=4] {'row'}, dimensions={0}, use_global_device_ids=true | all-gather | bytes 655360 | tf_op jit(solution)/shard_map/all_gather | solution.py:46
  300.9 23.5 %reduce-scatter.15.cloned.1.call-done = bf16[512,128]{1,0:T(8,128)(2,1)} async-done(((bf16[2048,128]{1,0:T(8,128)(2,1)}), bf16[512,128]{1,0:T(8,128)(2,1)}) %reduce-scatter.15.cloned.1.call-update) | async-done | bytes 131088 | tf_op jit(solution)/shard_map/reduce_scatter | solution.py:49
  331.0 14.9 %all_gather.38 = bf16[2048,128]{1,0:T(8,128)(2,1)S(1)} all-gather(bf16[512,128]{1,0:T(8,128)(2,1)S(1)} %fusion.20), channel_id=1, replica_groups=mesh['slab'=2,'row'=4,'col'=4] {'row'}, dimensions={0}, use_global_device_ids=true | all-gather | bytes 655360 | tf_op jit(solution)/shard_map/all_gather | solution.py:46
  352.5 23.5 %reduce-scatter.17.cloned.1.call-done = bf16[512,128]{1,0:T(8,128)(2,1)} async-done(((bf16[2048,128]{1,0:T(8,128)(2,1)}), bf16[512,128]{1,0:T(8,128)(2,1)}) %reduce-scatter.17.cloned.1.call-update) | async-done | bytes 131088 | tf_op jit(solution)/shard_map/reduce_scatter | solution.py:49
  382.5 14.9 %all_gather.39 = bf16[2048,128]{1,0:T(8,128)(2,1)S(1)} all-gather(bf16[512,128]{1,0:T(8,128)(2,1)S(1)} %fusion.21), channel_id=1, replica_groups=mesh['slab'=2,'row'=4,'col'=4] {'row'}, dimensions={0}, use_global_device_ids=true | all-gather | bytes 655360 | tf_op jit(solution)/shard_map/all_gather | solution.py:46
  404.0 23.5 %reduce-scatter.19.cloned.1.call-done = bf16[512,128]{1,0:T(8,128)(2,1)} async-done(((bf16[2048,128]{1,0:T(8,128)(2,1)}), bf16[512,128]{1,0:T(8,128)(2,1)}) %reduce-scatter.19.cloned.1.call-update) | async-done | bytes 131088 | tf_op jit(solution)/shard_map/reduce_scatter | solution.py:49
  434.1 14.9 %all_gather.40 = bf16[2048,128]{1,0:T(8,128)(2,1)S(1)} all-gather(bf16[512,128]{1,0:T(8,128)(2,1)S(1)} %fusion.22), channel_id=1, replica_groups=mesh['slab'=2,'row'=4,'col'=4] {'row'}, dimensions={0}, use_global_device_ids=true | all-gather | bytes 655360 | tf_op jit(solution)/shard_map/all_gather | solution.py:46
  462.4 16.8 %reduce-scatter.21.cloned.1.call-done = bf16[512,128]{1,0:T(8,128)(2,1)} async-done(((bf16[2048,128]{1,0:T(8,128)(2,1)}), bf16[512,128]{1,0:T(8,128)(2,1)}) %reduce-scatter.21.cloned.1.call-update) | async-done | bytes 131088 | tf_op jit(solution)/shard_map/reduce_scatter | solution.py:49
  490.1 21.8 %all_gather.41 = bf16[2048,128]{1,0:T(8,128)(2,1)S(1)} all-gather(bf16[512,128]{1,0:T(8,128)(2,1)S(1)} %fusion.23), channel_id=1, replica_groups=mesh['slab'=2,'row'=4,'col'=4] {'row'}, dimensions={0}, use_global_device_ids=true | all-gather | bytes 655360 | tf_op jit(solution)/shard_map/all_gather | solution.py:46
  520.7 18.9 %reduce-scatter.23.cloned.1.call-done = bf16[512,128]{0,1:T(8,128)(2,1)} async-done(((bf16[2048,128]{0,1:T(8,128)(2,1)}), bf16[512,128]{0,1:T(8,128)(2,1)}) %reduce-scatter.23.cloned.1.call-update) | async-done | bytes 131088 | tf_op jit(solution)/shard_map/reduce_scatter | solution.py:49
  (76 shorter events, 138.4 us)
Async XLA Ops:
  7.2 54.8 %reduce-scatter.25.cloned.1.call-start = ((), (), s32[]{:S(2)}) async-start(), calls=%async_computation.18 | async-start | bytes 655360 | tf_op jit(solution)/shard_map/reduce_scatter | solution.py:59
  31.6 37.4 %copy-start = (bf16[1,4,512,128]{3,2,1,0:T(8,128)(2,1)S(1)}, bf16[1,4,512,128]{3,2,1,0:T(8,128)(2,1)}, u32[]{:S(2)}) copy-start(bf16[1,4,512,128]{3,2,1,0:T(8,128)(2,1)} %param.5) | copy-start | bytes 1572868
  39.3 63.1 %reduce-scatter.27.cloned.1.call-start = ((), (), s32[]{:S(2)}) async-start(), calls=%async_computation.19 | async-start | bytes 655360 | tf_op jit(solution)/shard_map/reduce_scatter | solution.py:59
  61.9 7.1 %collective-permute-start.5 = (bf16[512,128]{1,0:T(8,128)(2,1)}, bf16[512,128]{1,0:T(8,128)(2,1)S(1)}, u32[]{:S(2)}, u32[]{:S(2)}) collective-permute-start(bf16[512,128]{1,0:T(8,128)(2,1)} %reduce-scatter.25.cloned.1.call-done), channel_id=1, source_target_pairs={{16,0},{17,1},{18,2},{19,3},{20,4},{21,5},{22,6},{23,7},{24,8},{25... | collective-permute-start | bytes 393224 | tf_op jit(solution)/shard_map/ppermute | solution.py:12
  83.8 59.1 %reduce-scatter.29.cloned.1.call-start = ((), (), s32[]{:S(2)}) async-start(), calls=%async_computation.20 | async-start | bytes 655360 | tf_op jit(solution)/shard_map/reduce_scatter | solution.py:59
  102.4 7.1 %collective-permute-start.6 = (bf16[512,128]{1,0:T(8,128)(2,1)}, bf16[512,128]{1,0:T(8,128)(2,1)S(1)}, u32[]{:S(2)}, u32[]{:S(2)}) collective-permute-start(bf16[512,128]{1,0:T(8,128)(2,1)} %reduce-scatter.27.cloned.1.call-done), channel_id=1, source_target_pairs={{16,0},{17,1},{18,2},{19,3},{20,4},{21,5},{22,6},{23,7},{24,8},{25... | collective-permute-start | bytes 393224 | tf_op jit(solution)/shard_map/ppermute | solution.py:12
  124.3 59.0 %reduce-scatter.31.cloned.1.call-start = ((), (), s32[]{:S(2)}) async-start(), calls=%async_computation.21 | async-start | bytes 655360 | tf_op jit(solution)/shard_map/reduce_scatter | solution.py:59
  142.9 7.1 %collective-permute-start.7 = (bf16[512,128]{1,0:T(8,128)(2,1)}, bf16[512,128]{1,0:T(8,128)(2,1)S(1)}, u32[]{:S(2)}, u32[]{:S(2)}) collective-permute-start(bf16[512,128]{1,0:T(8,128)(2,1)} %reduce-scatter.29.cloned.1.call-done), channel_id=1, source_target_pairs={{16,0},{17,1},{18,2},{19,3},{20,4},{21,5},{22,6},{23,7},{24,8},{25... | collective-permute-start | bytes 393224 | tf_op jit(solution)/shard_map/ppermute | solution.py:12
  164.8 59.1 %reduce-scatter.33.cloned.1.call-start = ((), (), s32[]{:S(2)}) async-start(), calls=%async_computation.22 | async-start | bytes 655360 | tf_op jit(solution)/shard_map/reduce_scatter | solution.py:59
  183.3 7.1 %collective-permute-start.8 = (bf16[512,128]{1,0:T(8,128)(2,1)}, bf16[512,128]{1,0:T(8,128)(2,1)S(1)}, u32[]{:S(2)}, u32[]{:S(2)}) collective-permute-start(bf16[512,128]{1,0:T(8,128)(2,1)} %reduce-scatter.31.cloned.1.call-done), channel_id=1, source_target_pairs={{16,0},{17,1},{18,2},{19,3},{20,4},{21,5},{22,6},{23,7},{24,8},{25... | collective-permute-start | bytes 393224 | tf_op jit(solution)/shard_map/ppermute | solution.py:12
  205.3 67.6 %reduce-scatter.13.cloned.1.call-start = ((), (), s32[]{:S(2)}) async-start(), calls=%async_computation.12 | async-start | bytes 655360 | tf_op jit(solution)/shard_map/reduce_scatter | solution.py:49
  223.9 7.1 %collective-permute-start.9 = (bf16[512,128]{1,0:T(8,128)(2,1)}, bf16[512,128]{1,0:T(8,128)(2,1)S(1)}, u32[]{:S(2)}, u32[]{:S(2)}) collective-permute-start(bf16[512,128]{1,0:T(8,128)(2,1)} %reduce-scatter.33.cloned.1.call-done), channel_id=1, source_target_pairs={{16,0},{17,1},{18,2},{19,3},{20,4},{21,5},{22,6},{23,7},{24,8},{25... | collective-permute-start | bytes 393224 | tf_op jit(solution)/shard_map/ppermute | solution.py:12
  252.6 71.8 %reduce-scatter.15.cloned.1.call-start = ((), (), s32[]{:S(2)}) async-start(), calls=%async_computation.13 | async-start | bytes 655360 | tf_op jit(solution)/shard_map/reduce_scatter | solution.py:49
  272.9 6.4 %collective-permute-start = (bf16[512,128]{1,0:T(8,128)(2,1)}, bf16[512,128]{1,0:T(8,128)(2,1)S(1)}, u32[]{:S(2)}, u32[]{:S(2)}) collective-permute-start(bf16[512,128]{1,0:T(8,128)(2,1)} %reduce-scatter.13.cloned.1.call-done), channel_id=1, source_target_pairs={{0,16},{1,17},{2,18},{3,19},{4,20},{5,21},{6,22},{7,23},{8,24},{9,... | collective-permute-start | bytes 393224 | tf_op jit(solution)/shard_map/ppermute | solution.py:12
  300.9 75.1 %reduce-scatter.17.cloned.1.call-start = ((), (), s32[]{:S(2)}) async-start(), calls=%async_computation.14 | async-start | bytes 655360 | tf_op jit(solution)/shard_map/reduce_scatter | solution.py:49
  324.4 6.4 %collective-permute-start.1 = (bf16[512,128]{1,0:T(8,128)(2,1)}, bf16[512,128]{1,0:T(8,128)(2,1)S(1)}, u32[]{:S(2)}, u32[]{:S(2)}) collective-permute-start(bf16[512,128]{1,0:T(8,128)(2,1)} %reduce-scatter.15.cloned.1.call-done), channel_id=1, source_target_pairs={{0,16},{1,17},{2,18},{3,19},{4,20},{5,21},{6,22},{7,23},{8,24},{9,... | collective-permute-start | bytes 393224 | tf_op jit(solution)/shard_map/ppermute | solution.py:12
  352.4 75.1 %reduce-scatter.19.cloned.1.call-start = ((), (), s32[]{:S(2)}) async-start(), calls=%async_computation.15 | async-start | bytes 655360 | tf_op jit(solution)/shard_map/reduce_scatter | solution.py:49
  376.0 6.4 %collective-permute-start.2 = (bf16[512,128]{1,0:T(8,128)(2,1)}, bf16[512,128]{1,0:T(8,128)(2,1)S(1)}, u32[]{:S(2)}, u32[]{:S(2)}) collective-permute-start(bf16[512,128]{1,0:T(8,128)(2,1)} %reduce-scatter.17.cloned.1.call-done), channel_id=1, source_target_pairs={{0,16},{1,17},{2,18},{3,19},{4,20},{5,21},{6,22},{7,23},{8,24},{9,... | collective-permute-start | bytes 393224 | tf_op jit(solution)/shard_map/ppermute | solution.py:12
  404.0 75.1 %reduce-scatter.21.cloned.1.call-start = ((), (), s32[]{:S(2)}) async-start(), calls=%async_computation.16 | async-start | bytes 655360 | tf_op jit(solution)/shard_map/reduce_scatter | solution.py:49
  427.5 6.4 %collective-permute-start.3 = (bf16[512,128]{1,0:T(8,128)(2,1)}, bf16[512,128]{1,0:T(8,128)(2,1)S(1)}, u32[]{:S(2)}, u32[]{:S(2)}) collective-permute-start(bf16[512,128]{1,0:T(8,128)(2,1)} %reduce-scatter.19.cloned.1.call-done), channel_id=1, source_target_pairs={{0,16},{1,17},{2,18},{3,19},{4,20},{5,21},{6,22},{7,23},{8,24},{9,... | collective-permute-start | bytes 393224 | tf_op jit(solution)/shard_map/ppermute | solution.py:12
  455.5 63.5 %reduce-scatter.35.cloned.1.call-start = ((), (), s32[]{:S(2)}) async-start(), calls=%async_computation.23 | async-start | bytes 655360 | tf_op jit(solution)/shard_map/reduce_scatter | solution.py:59
  479.1 10.8 %collective-permute-start.4 = (bf16[512,128]{1,0:T(8,128)(2,1)}, bf16[512,128]{1,0:T(8,128)(2,1)S(1)}, u32[]{:S(2)}, u32[]{:S(2)}) collective-permute-start(bf16[512,128]{1,0:T(8,128)(2,1)} %reduce-scatter.21.cloned.1.call-done), channel_id=1, source_target_pairs={{0,16},{1,17},{2,18},{3,19},{4,20},{5,21},{6,22},{7,23},{8,24},{9,... | collective-permute-start | bytes 393224 | tf_op jit(solution)/shard_map/ppermute | solution.py:12
  488.0 51.5 %reduce-scatter.23.cloned.1.call-start = ((), (), s32[]{:S(2)}) async-start(), calls=%async_computation.17 | async-start | bytes 655360 | tf_op jit(solution)/shard_map/reduce_scatter | solution.py:49
Sparse Core Ops, SparseCore 0:
  39.4 22.5 reduce-scatter.24
  83.9 18.4 reduce-scatter.26
  124.4 18.4 reduce-scatter.28
  164.9 18.4 reduce-scatter.30
  205.4 18.4 reduce-scatter.32
  252.7 20.0 reduce-scatter.12
  301.0 23.3 reduce-scatter.14
  352.6 23.3 reduce-scatter.16
  404.1 23.3 reduce-scatter.18
  455.7 23.4 reduce-scatter.20
  488.1 23.6 reduce-scatter.34
  519.1 20.4 reduce-scatter.22
where the time goes:
time: 558 us; the launch traced here: 549 us
  waiting for transfers between devices  245 us (44%)
  blocking collectives  140 us (25%)
  matrix products  83.3 us (15%)
  between operations  37.9 us (7%)
  starting transfers between devices  23.9 us (4%)
  local copies, waits for them, and re-layouts  16.1 us (3%)
    reduce_scatter x6, waiting for transfers between devices, per_device(): lax.psum_scatter(forward_partial_value.astype(jnp.bfloat16), 'col', scatt...  126 us
    all_gather x6, blocking collectives, per_device(): lax.all_gather(up_in, 'row', axis=0, tiled=True)  96.2 us
    reduce_scatter x6, waiting for transfers between devices, per_device(): lax.psum_scatter(partial_value.astype(jnp.bfloat16), 'row', scatter_dimen...  92.9 us
    all_gather x6, blocking collectives, per_device(): lax.all_gather(down_in, 'col', axis=0, tiled=True)  43.8 us
    dot_general x6, matrix products, per_device(): lax.dot_general(matrix, lax.all_gather(down_in, 'col', axis=0, tiled=True...  43.5 us
    dot_general x6, matrix products, per_device(): jnp.dot(matrix, lax.all_gather(up_in, 'row', axis=0, tiled=True), preferr...  39.9 us
    ppermute x10, waiting for transfers between devices, shifted(): lax.ppermute(value, axis, [(source, source + steps) for source in range(l...  25.4 us
    ppermute x10, starting transfers between devices, shifted(): lax.ppermute(value, axis, [(source, source + steps) for source in range(l...  23.4 us
  transfers between devices with their start and end apart: 22, of which 20 were waited for; matrix products, arithmetic and copies ran while one was open for 3% of the time, Pallas kernels for 0%

commit v1 on v0

v1 whole, which is shorter than its diff:
```python
import functools

import jax
import jax.numpy as jnp
from jax import lax
from jax.experimental import pallas as pl
from jax.experimental.pallas import tpu as pltpu
from jax.sharding import PartitionSpec as P

TICKS = 6
MESH = pl.DeviceIdType.MESH
f32 = jnp.float32
bf16 = jnp.bfloat16


def shifted(value, axis, steps):
    count = lax.axis_size(axis)
    leading, last = (max(0, -steps), min(count, count - steps))
    return lax.ppermute(value, axis, [(source, source + steps) for source in range(leading, last)])


def tick_by_tick(inverse, sources, coupling, plan):
    local_block = inverse[0]
    matrix = local_block.reshape(local_block.shape[0], -1)
    piece_rows, batch_width = sources.shape[2:]
    slab_index = lax.axis_index("slab")
    up_gain = coupling[0, 0][:, None]
    down_gain = coupling[0, 1][:, None]
    stored = sources[0]
    up_out = jnp.zeros((piece_rows, batch_width), bf16)
    down_out = jnp.zeros((piece_rows, batch_width), bf16)
    for tick in range(TICKS):
        up_recv, down_recv = up_out, down_out
        if tick:
            up_recv = shifted(up_out, "slab", 1)
            down_recv = shifted(down_out, "slab", -1)
        up_source = lax.dynamic_index_in_dim(stored, plan[tick, slab_index, 0], 0, keepdims=False)
        down_source = lax.dynamic_index_in_dim(stored, plan[tick, slab_index, 1], 0, keepdims=False)
        up_in = (up_source.astype(f32) + up_gain * up_recv.astype(f32)).astype(bf16)
        down_in = (down_source.astype(f32) + down_gain * down_recv.astype(f32)).astype(bf16)
        up_part = jnp.dot(matrix, lax.all_gather(up_in, "row", axis=0, tiled=True), preferred_element_type=f32)
        up_out = lax.psum_scatter(up_part.astype(bf16), "col", scatter_dimension=0, tiled=True)
        down_part = lax.dot_general(
            matrix,
            lax.all_gather(down_in, "col", axis=0, tiled=True),
            (((0,), (0,)), ((), ())),
            preferred_element_type=f32,
        )
        down_out = lax.psum_scatter(down_part.astype(bf16), "row", scatter_dimension=0, tiled=True)
    return (up_out[None], down_out[None])


def sweep_kernel(
    R, C, NB, T,
    plan, g, src, src_t, gain_up, gain_down,
    up_out, down_out,
    ux, up_part, up_got, up_first, up_second, up_in,
    dx, dn_part, dn_right, dn_left, dn_from_left, dn_from_right, dn_first, dn_second, dn_in,
    ux_s, ux_r, up_s, up_r, uy_s, uy_r,
    dx_s, dx_r, dr_s, dr_r, dl_s, dl_r, dy_s, dy_r,
):
    slab, r, c = lax.axis_index("slab"), lax.axis_index("row"), lax.axis_index("col")
    other = 1 - slab
    n, b = src.shape[1], src.shape[2]

    barrier = pltpu.get_barrier_semaphore()
    for step in (1, R - 1):
        pl.semaphore_signal(barrier, inc=1, device_id={"row": lax.rem(r + step, R)}, device_id_type=MESH)
    for step in range(1, C):
        pl.semaphore_signal(barrier, inc=1, device_id={"col": lax.rem(c + step, C)}, device_id_type=MESH)
    pl.semaphore_signal(barrier, inc=1, device_id={"slab": other}, device_id_type=MESH)
    pl.semaphore_wait(barrier, 2 + (C - 1) + 1)

    def remote(source, target, send, recv, **where):
        return pltpu.make_async_remote_copy(
            src_ref=source, dst_ref=target, send_sem=send, recv_sem=recv, device_id=where, device_id_type=MESH
        )

    def ux_copy(u, k, way):
        to = jnp.minimum(r + 1, R - 1) if way else jnp.maximum(r - 1, 0)
        return remote(ux.at[u, k], ux.at[u, k], ux_s.at[u, k, way], ux_r.at[u, k], row=to)

    def up_copy(u, to):
        return remote(up_part.at[u, to], up_got.at[u, c], up_s.at[u, to], up_r.at[u, c], col=to)

    def up_got_copy(u, origin):
        return remote(up_part.at[u, origin], up_got.at[u, origin], up_s.at[u, origin], up_r.at[u, origin], col=origin)

    def uy_copy(u):
        return remote(up_first.at[u], up_in.at[u], uy_s.at[u], uy_r.at[u], slab=other)

    def dx_copy(u, to):
        return remote(dx.at[u, c], dx.at[u, c], dx_s.at[u, to], dx_r.at[u, c], col=to)

    def dx_got_copy(u, origin):
        return remote(dx.at[u, origin], dx.at[u, origin], dx_s.at[u, origin], dx_r.at[u, origin], col=origin)

    def dr_copy(u, d):
        return remote(dn_right.at[u, d], dn_from_left.at[u, d], dr_s.at[u, d], dr_r.at[u, d], row=jnp.minimum(r + 1, R - 1))

    def dl_copy(u, d):
        return remote(dn_left.at[u, d], dn_from_right.at[u, d], dl_s.at[u, d], dl_r.at[u, d], row=jnp.maximum(r - 1, 0))

    def dy_copy(u):
        return remote(dn_first.at[u], dn_in.at[u], dy_s.at[u], dy_r.at[u], slab=other)

    def formed(source, gain, prev):
        return (source.astype(f32) + gain * prev.astype(f32)).astype(bf16)

    def up_form(phase, units):
        @pl.when(phase == 0)
        def _():
            @pl.loop(0, NB)
            def _(u):
                ux[u, r] = formed(src[u], gain_up[...], jnp.zeros((n, b), bf16))

        @pl.when(phase == 1)
        def _():
            @pl.loop(0, NB)
            def _(u):
                uy_copy(u).wait_recv()

            @pl.loop(0, T)
            def _(t):
                prev = up_in[plan[jnp.maximum(t - 1, 0), other, 0]].astype(f32)
                prev = jnp.where(t > 0, prev, 0.0)
                ux[t, r] = formed(src[plan[t, slab, 0]], gain_up[...], prev)

    def up_sweep(phase, units):
        up_form(phase, units)

        def own(u):
            @pl.when(r < R - 1)
            def _():
                ux_copy(u, r, 1).start()

            @pl.when(r > 0)
            def _():
                ux_copy(u, r, 0).start()

        own(0)
        own(1)

        @pl.loop(0, units + 1)
        def _(i):
            @pl.when(i < units)
            def _():
                for d in range(1, R):
                    @pl.when(r - d >= 0)
                    def _():
                        ux_copy(i, r - d, 1).wait_recv()

                        @pl.when(r < R - 1)
                        def _():
                            ux_copy(i, r - d, 1).start()

                    @pl.when(r + d < R)
                    def _():
                        ux_copy(i, r + d, 0).wait_recv()

                        @pl.when(r > 0)
                        def _():
                            ux_copy(i, r + d, 0).start()

                @pl.when(i + 2 < units)
                def _():
                    own(i + 2)

                @pl.loop(1, C + 1)
                def _(j):
                    to = lax.rem(c + j, C)
                    x = ux[i].reshape(R * n, b)
                    rows = pl.ds(pl.multiple_of(to * n, n), n)
                    up_part[i, to] = jnp.dot(g[rows, :], x, preferred_element_type=f32).astype(bf16)

                    @pl.when(j < C)
                    def _():
                        up_copy(i, to).start()

            @pl.when(i > 0)
            def _():
                u = i - 1
                total = up_part[u, c].astype(f32)
                for j in range(1, C):
                    origin = lax.rem(c + j, C)
                    up_got_copy(u, origin).wait_recv()
                    total = total + up_got[u, origin].astype(f32)

                @pl.when(phase == 0)
                def _():
                    up_first[u] = total.astype(bf16)
                    uy_copy(u).start()

                @pl.when(phase == 1)
                def _():
                    up_second[u] = total.astype(bf16)

    def up_drain(phase, units):
        @pl.loop(0, units)
        def _(u):
            for k in range(R):
                @pl.when(jnp.logical_and(r < R - 1, k <= r))
                def _():
                    ux_copy(u, k, 1).wait_send()

                @pl.when(jnp.logical_and(r > 0, k >= r))
                def _():
                    ux_copy(u, k, 0).wait_send()

            for j in range(1, C):
                up_copy(u, lax.rem(c + j, C)).wait_send()

            @pl.when(phase == 0)
            def _():
                uy_copy(u).wait_send()

    def down_form(phase, units):
        @pl.when(phase == 0)
        def _():
            @pl.loop(0, NB)
            def _(u):
                dx[u, c] = formed(src_t[u], gain_down[...], jnp.zeros((b, n), bf16))
                for j in range(1, C):
                    dx_copy(u, lax.rem(c + j, C)).start()

        @pl.when(phase == 1)
        def _():
            @pl.loop(0, NB)
            def _(u):
                dy_copy(u).wait_recv()

            @pl.loop(0, T)
            def _(t):
                prev = dn_in[plan[jnp.maximum(t - 1, 0), other, 1]].astype(f32)
                prev = jnp.where(t > 0, prev, 0.0)
                dx[t, c] = formed(src_t[plan[t, slab, 1]], gain_down[...], prev)
                for j in range(1, C):
                    dx_copy(t, lax.rem(c + j, C)).start()

    def down_sweep(phase, units):
        down_form(phase, units)

        @pl.loop(0, units + R - 1)
        def _(i):
            @pl.when(i < units)
            def _():
                for j in range(1, C):
                    dx_got_copy(i, lax.rem(c + j, C)).wait_recv()

                @pl.loop(0, R)
                def _(k):
                    cols = pl.ds(pl.multiple_of(k * n, n), n)
                    total = jnp.dot(dx[i, 0], g[0:n, cols], preferred_element_type=f32)
                    for q in range(1, C):
                        total += jnp.dot(dx[i, q], g[q * n:(q + 1) * n, cols], preferred_element_type=f32)
                    dn_part[i, k] = total.astype(bf16)

            ur = i - r

            @pl.when(jnp.logical_and(r < R - 1, jnp.logical_and(ur >= 0, ur < units)))
            def _():
                for d in reversed(range(1, R)):
                    @pl.when(d > r)
                    def _():
                        @pl.when(r == 0)
                        def _():
                            dn_right[ur, d] = dn_part[ur, d]

                        @pl.when(r > 0)
                        def _():
                            dr_copy(ur, d).wait_recv()
                            dn_right[ur, d] = (dn_part[ur, d].astype(f32) + dn_from_left[ur, d].astype(f32)).astype(bf16)

                        dr_copy(ur, d).start()

            ul = i - (R - 1 - r)

            @pl.when(jnp.logical_and(r > 0, jnp.logical_and(ul >= 0, ul < units)))
            def _():
                for d in range(R - 1):
                    @pl.when(d < r)
                    def _():
                        @pl.when(r == R - 1)
                        def _():
                            dn_left[ul, d] = dn_part[ul, d]

                        @pl.when(r < R - 1)
                        def _():
                            dl_copy(ul, d).wait_recv()
                            dn_left[ul, d] = (dn_part[ul, d].astype(f32) + dn_from_right[ul, d].astype(f32)).astype(bf16)

                        dl_copy(ul, d).start()

            @pl.when(i >= R - 1)
            def _():
                u = i - (R - 1)

                def finish(total):
                    @pl.when(phase == 0)
                    def _():
                        dn_first[u] = total.astype(bf16)
                        dy_copy(u).start()

                    @pl.when(phase == 1)
                    def _():
                        dn_second[u] = total.astype(bf16)

                @pl.when(r > 0)
                def _():
                    dr_copy(u, r).wait_recv()

                @pl.when(r < R - 1)
                def _():
                    dl_copy(u, r).wait_recv()

                mine = dn_part[u, r].astype(f32)

                @pl.when(r == 0)
                def _():
                    finish(mine + dn_from_right[u, r].astype(f32))

                @pl.when(r == R - 1)
                def _():
                    finish(mine + dn_from_left[u, r].astype(f32))

                @pl.when(jnp.logical_and(r > 0, r < R - 1))
                def _():
                    finish(mine + dn_from_left[u, r].astype(f32) + dn_from_right[u, r].astype(f32))

    def down_drain(phase, units):
        @pl.loop(0, units)
        def _(u):
            for j in range(1, C):
                dx_copy(u, lax.rem(c + j, C)).wait_send()
            for d in range(R):
                @pl.when(d > r)
                def _():
                    dr_copy(u, d).wait_send()

                @pl.when(d < r)
                def _():
                    dl_copy(u, d).wait_send()

            @pl.when(phase == 0)
            def _():
                dy_copy(u).wait_send()

    @pl.loop(0, 2)
    def _(phase):
        units = jnp.where(phase == 0, NB, T)
        upward = lax.rem(phase + slab, 2) == 0

        @pl.when(upward)
        def _():
            up_sweep(phase, units)
            up_drain(phase, units)

        @pl.when(jnp.logical_not(upward))
        def _():
            down_sweep(phase, units)
            down_drain(phase, units)

    @pl.when(slab == 0)
    def _():
        up_out[...] = up_first[plan[T - 1, slab, 0]]
        down_out[...] = dn_second[T - 1]

    @pl.when(slab == 1)
    def _():
        up_out[...] = up_second[T - 1]
        down_out[...] = dn_first[plan[T - 1, slab, 1]]


def two_slabs(R, C, inverse, sources, coupling, plan):
    matrix = inverse[0].reshape(inverse.shape[1], -1)
    src = sources[0]
    NB, n, b = src.shape
    T = TICKS
    V = lambda *shape: pltpu.VMEM(shape, bf16)
    D = lambda *shape: pltpu.SemaphoreType.DMA(shape)
    vmem = pl.BlockSpec(memory_space=pltpu.VMEM)
    flops = 2 * matrix.size * b * (NB + T)
    up, down_t = pl.pallas_call(
        functools.partial(sweep_kernel, R, C, NB, T),
        out_shape=(jax.ShapeDtypeStruct((n, b), bf16), jax.ShapeDtypeStruct((b, n), bf16)),
        in_specs=[pl.BlockSpec(memory_space=pltpu.SMEM)] + [vmem] * 5,
        out_specs=(vmem, vmem),
        scratch_shapes=[
            V(T, R, n, b), V(T, C, n, b), V(T, C, n, b), V(NB, n, b), V(T, n, b), V(NB, n, b),
            V(T, C, b, n), V(T, R, b, n), V(T, R, b, n), V(T, R, b, n), V(T, R, b, n), V(T, R, b, n),
            V(NB, b, n), V(T, b, n), V(NB, b, n),
            D(T, R, 2), D(T, R), D(T, C), D(T, C), D(NB), D(NB),
            D(T, C), D(T, C), D(T, R), D(T, R), D(T, R), D(T, R), D(NB), D(NB),
        ],
        compiler_params=pltpu.CompilerParams(
            collective_id=0, has_side_effects=True, vmem_limit_bytes=56 * 1024 * 1024
        ),
        cost_estimate=pl.CostEstimate(flops=flops, bytes_accessed=2 * matrix.size, transcendentals=0),
    )(
        plan, matrix, src, jnp.swapaxes(src, 1, 2), coupling[0, 0][:, None], coupling[0, 1][None, :],
    )
    return up[None], down_t.T[None]


def solution(mesh):
    placed = (
        P("slab", "row", None, "col"),
        P("slab", None, ("row", "col"), None),
        P("slab", None, ("row", "col")),
        P(),
    )
    sizes = mesh.shape
    body = tick_by_tick
    if sizes["slab"] == 2 and sizes["row"] > 2 and sizes["col"] > 1:
        body = functools.partial(two_slabs, sizes["row"], sizes["col"])
    return jax.shard_map(
        body,
        mesh=mesh,
        in_specs=placed,
        out_specs=(P("slab", ("row", "col"), None), P("slab", ("row", "col"), None)),
        check_vma=False,
    )
```

time: 558 us -> 146 us (0.26); the launches traced: 549 us -> 143 us
  waiting for transfers between devices: 245 us -> 0 us
  blocking collectives: 140 us -> 0 us
  Pallas kernels: 0 us -> 124 us
  matrix products: 83.3 us -> 0 us
  between operations: 37.9 us -> 0.64 us
  starting transfers between devices: 23.9 us -> 0 us
    reduce_scatter x12 -> x0, waiting for transfers between devices: 219 us -> none  [the longest x6 126 us: per_device(): lax.psum_scatter(forward_partial_value.astype(jnp.bfloat16), 'col', scatt...]
    all_gather x12 -> x0, blocking collectives: 140 us -> none  [the longest x6 96.2 us: per_device(): lax.all_gather(up_in, 'row', axis=0, tiled=True)]
    pallas_call x0 -> x1, Pallas kernels: none -> 124 us  [two_slabs(): pl.pallas_call(functools.partial(sweep_kernel, R, C, NB, T), out_shape=(j...]
    dot_general x12 -> x0, matrix products: 83.3 us -> none  [the longest x6 43.5 us: per_device(): lax.dot_general(matrix, lax.all_gather(down_in, 'col', axis=0, tiled=True...]
    ppermute x10 -> x0, waiting for transfers between devices: 25.4 us -> none  [shifted(): lax.ppermute(value, axis, [(source, source + steps) for source in range(l...]
    ppermute x10 -> x0, starting transfers between devices: 23.4 us -> none  [shifted(): lax.ppermute(value, axis, [(source, source + steps) for source in range(l...]
  transfers between devices with their start and end apart: 22 -> 0, of which waited for: 20 -> 0; matrix products, arithmetic and copies ran while one was open for 3% -> 0% of each run, Pallas kernels for 0% -> 0%
where the time goes in v1:
time: 146 us; the launch traced here: 143 us
  Pallas kernels  124 us (85%)
  local copies, waits for them, and re-layouts  19.1 us (13%)
    pallas_call x1, Pallas kernels, two_slabs(): pl.pallas_call(functools.partial(sweep_kernel, R, C, NB, T), out_shape=(j...  124 us
    unnamed x5, local copies, waits for them, and re-layouts  16.9 us

profile of v1, /device:TPU:0, one launch (start us, length us, event | category | flops | bytes accessed | tf_op | source)
XLA Modules:
  0.0 143.3 jit_solution(952831415234240672)
XLA Ops:
  0.6 1.3 slice_bitcast_fusion
  2.0 1.4 copy.11.plan
  3.3 0.9 copy.13.gain_up
  4.2 2.1 %copy.10 = bf16[1,4,512,128]{2,3,1,0:T(8,128)(2,1)} copy(bf16[1,4,512,128]{3,2,1,0:T(8,128)(2,1)} %param.5) | data formatting | bytes 1048576 | tf_op args[1]
  6.3 10.2 %copy.16 = bf16[256,8,4,512]{3,1,2,0:T(8,128)(2,1)} copy(bf16[256,8,4,512]{3,2,1,0:T(4,128)(2,1)} %bitcast.15) | data formatting | bytes 16777216
  16.5 123.5 %shard_map.59 = (bf16[512,128]{1,0:T(8,128)(2,1)}, bf16[128,512]{1,0:T(8,128)(2,1)}) custom-call(s32[6,2,2]{2,1,0:T(2,128)} %copy.11.plan, bf16[2048,2048]{1,0:T(8,128)(2,1)} %bitcast.16, bf16[4,512,128]{2,1,0:T(8,128)(2,1)} %bitcast.17, bf16[4,128,512]{2,1,0:T(8,128)(2,1)} %bitcast.18, f32[512,1]{1,0:T(8,128)} %copy.13.gain_up, ...), custom_call_target="tpu_custom_call" | custom-call | flops 10737418240 | bytes 8388608 | tf_op jit(solution)/shard_map/pallas_call | solution.py:383
  140.1 1.7 %copy.14 = bf16[1,512,128]{2,1,0:T(8,128)(2,1)} copy(bf16[1,512,128]{1,2,0:T(8,128)(2,1)} %bitcast.20) | data formatting | bytes 262144
  141.7 1.6 %copy.18 = bf16[1,512,128]{2,1,0:T(8,128)(2,1)} copy(bf16[1,512,128]{2,1,0:T(8,128)(2,1)} %bitcast.19) | data formatting | bytes 262144

commit v2 on v1

--- a/solution.py
+++ b/solution.py
@@ -54,14 +54,17 @@
     R, C, NB, T,
     plan, g, src, src_t, gain_up, gain_down,
     up_out, down_out,
-    ux, up_part, up_got, up_first, up_second, up_in,
+    ux, up_part, up_got, up_mid, up_first, up_second, up_in,
     dx, dn_part, dn_right, dn_left, dn_from_left, dn_from_right, dn_first, dn_second, dn_in,
     ux_s, ux_r, up_s, up_r, uy_s, uy_r,
     dx_s, dx_r, dr_s, dr_r, dl_s, dl_r, dy_s, dy_r,
+    mid_s, mid_r, pass_s,
 ):
     slab, r, c = lax.axis_index("slab"), lax.axis_index("row"), lax.axis_index("col")
     other = 1 - slab
     n, b = src.shape[1], src.shape[2]
+    sib = c + 1 - 2 * lax.rem(c, 2)
+    far = [lax.rem(c + j, C) for j in range(2, C, 2)]
 
     barrier = pltpu.get_barrier_semaphore()
     for step in (1, R - 1):
@@ -86,11 +89,17 @@
     def up_got_copy(u, origin):
         return remote(up_part.at[u, origin], up_got.at[u, origin], up_s.at[u, origin], up_r.at[u, origin], col=origin)
 
+    def mid_copy(u, dest):
+        return remote(up_part.at[u, dest], up_mid.at[u, dest], mid_s.at[u, dest], mid_r.at[u, dest], col=sib)
+
     def uy_copy(u):
         return remote(up_first.at[u], up_in.at[u], uy_s.at[u], uy_r.at[u], slab=other)
 
     def dx_copy(u, to):
         return remote(dx.at[u, c], dx.at[u, c], dx_s.at[u, to], dx_r.at[u, c], col=to)
+
+    def pass_copy(u, origin):
+        return remote(dx.at[u, origin], dx.at[u, origin], pass_s.at[u, origin], dx_r.at[u, origin], col=sib)
 
     def dx_got_copy(u, origin):
         return remote(dx.at[u, origin], dx.at[u, origin], dx_s.at[u, origin], dx_r.at[u, origin], col=origin)
@@ -120,69 +129,91 @@
             def _(u):
                 uy_copy(u).wait_recv()
 
-            @pl.loop(0, T)
+            @pl.loop(1, T)
             def _(t):
-                prev = up_in[plan[jnp.maximum(t - 1, 0), other, 0]].astype(f32)
-                prev = jnp.where(t > 0, prev, 0.0)
+                prev = up_in[plan[t - 1, other, 0]]
                 ux[t, r] = formed(src[plan[t, slab, 0]], gain_up[...], prev)
+
+    def own(u):
+        @pl.when(r < R - 1)
+        def _():
+            ux_copy(u, r, 1).start()
+
+        @pl.when(r > 0)
+        def _():
+            ux_copy(u, r, 0).start()
 
     def up_sweep(phase, units):
         up_form(phase, units)
 
-        def own(u):
-            @pl.when(r < R - 1)
-            def _():
-                ux_copy(u, r, 1).start()
-
-            @pl.when(r > 0)
-            def _():
-                ux_copy(u, r, 0).start()
-
-        own(0)
-        own(1)
-
-        @pl.loop(0, units + 1)
+        @pl.when(phase == 0)
+        def _():
+            own(0)
+
+        @pl.loop(0, units + R - 1)
         def _(i):
-            @pl.when(i < units)
-            def _():
-                for d in range(1, R):
+            @pl.when(i + 1 < units)
+            def _():
+                own(i + 1)
+
+            for d in reversed(range(1, R)):
+                u = i - (d - 1)
+
+                @pl.when(jnp.logical_and(u >= 0, u < units))
+                def _():
                     @pl.when(r - d >= 0)
                     def _():
-                        ux_copy(i, r - d, 1).wait_recv()
+                        ux_copy(u, r - d, 1).wait_recv()
 
                         @pl.when(r < R - 1)
                         def _():
-                            ux_copy(i, r - d, 1).start()
+                            ux_copy(u, r - d, 1).start()
 
                     @pl.when(r + d < R)
                     def _():
-                        ux_copy(i, r + d, 0).wait_recv()
+                        ux_copy(u, r + d, 0).wait_recv()
 
                         @pl.when(r > 0)
                         def _():
-                            ux_copy(i, r + d, 0).start()
-
-                @pl.when(i + 2 < units)
-                def _():
-                    own(i + 2)
-
-                @pl.loop(1, C + 1)
+                            ux_copy(u, r + d, 0).start()
+
+            um = i - (R - 2)
+
+            @pl.when(jnp.logical_and(um >= 0, um < units))
+            def _():
+                @pl.loop(1, C // 2 + 1)
                 def _(j):
-                    to = lax.rem(c + j, C)
-                    x = ux[i].reshape(R * n, b)
+                    to = lax.rem(sib + 2 * j, C)
                     rows = pl.ds(pl.multiple_of(to * n, n), n)
-                    up_part[i, to] = jnp.dot(g[rows, :], x, preferred_element_type=f32).astype(bf16)
-
-                    @pl.when(j < C)
-                    def _():
-                        up_copy(i, to).start()
-
-            @pl.when(i > 0)
-            def _():
-                u = i - 1
+                    x = ux[um].reshape(R * n, b)
+                    up_part[um, to] = jnp.dot(g[rows, :], x, preferred_element_type=f32).astype(bf16)
+
+                    @pl.when(j < C // 2)
+                    def _():
+                        mid_copy(um, to).start()
+
+                    @pl.when(j == C // 2)
+                    def _():
+                        up_copy(um, sib).start()
+
+                @pl.loop(1, C // 2 + 1)
+                def _(j):
+                    to = lax.rem(c + 2 * j, C)
+                    rows = pl.ds(pl.multiple_of(to * n, n), n)
+                    x = ux[um].reshape(R * n, b)
+                    up_part[um, to] = jnp.dot(g[rows, :], x, preferred_element_type=f32).astype(bf16)
+
+                    @pl.when(j < C // 2)
+                    def _():
+                        mid_copy(um, to).wait_recv()
+                        up_part[um, to] = (up_part[um, to].astype(f32) + up_mid[um, to].astype(f32)).astype(bf16)
+                        up_copy(um, to).start()
+
+            @pl.when(i >= R - 1)
+            def _():
+                u = i - (R - 1)
                 total = up_part[u, c].astype(f32)
-                for j in range(1, C):
-                    origin = lax.rem(c + j, C)
+                for origin in [sib] + far:
                     up_got_copy(u, origin).wait_recv()
                     total = total + up_got[u, origin].astype(f32)
 
@@ -207,8 +238,10 @@
                 def _():
                     ux_copy(u, k, 0).wait_send()
 
-            for j in range(1, C):
-                up_copy(u, lax.rem(c + j, C)).wait_send()
+            for to in [sib] + far:
+                up_copy(u, to).wait_send()
+            for j in range(2, C, 2):
+                mid_copy(u, lax.rem(sib + j, C)).wait_send()
 
             @pl.when(phase == 0)
             def _():
@@ -220,22 +253,20 @@
             @pl.loop(0, NB)
             def _(u):
                 dx[u, c] = formed(src_t[u], gain_down[...], jnp.zeros((b, n), bf16))
-                for j in range(1, C):
-                    dx_copy(u, lax.rem(c + j, C)).start()
-
-        @pl.when(phase == 1)
-        def _():
-            @pl.loop(0, NB)
-            def _(u):
-                dy_copy(u).wait_recv()
-
-            @pl.loop(0, T)
-            def _(t):
-                prev = dn_in[plan[jnp.maximum(t - 1, 0), other, 1]].astype(f32)
-                prev = jnp.where(t > 0, prev, 0.0)
-                dx[t, c] = formed(src_t[plan[t, slab, 1]], gain_down[...], prev)
-                for j in range(1, C):
-                    dx_copy(t, lax.rem(c + j, C)).start()
+                for to in far + [sib]:
+                    dx_copy(u, to).start()
+
+    def down_rest():
+        @pl.loop(0, NB)
+        def _(u):
+            dy_copy(u).wait_recv()
+
+        @pl.loop(1, T)
+        def _(t):
+            prev = dn_in[plan[t - 1, other, 1]]
+            dx[t, c] = formed(src_t[plan[t, slab, 1]], gain_down[...], prev)
+            for to in far + [sib]:
+                dx_copy(t, to).start()
 
     def down_sweep(phase, units):
         down_form(phase, units)
@@ -244,8 +275,11 @@
         def _(i):
             @pl.when(i < units)
             def _():
-                for j in range(1, C):
-                    dx_got_copy(i, lax.rem(c + j, C)).wait_recv()
+                for origin in far:
+                    dx_got_copy(i, origin).wait_recv()
+                    pass_copy(i, origin).start()
+                for origin in [sib] + [lax.rem(sib + j, C) for j in range(2, C, 2)]:
+                    dx_got_copy(i, origin).wait_recv()
 
                 @pl.loop(0, R)
                 def _(k):
@@ -255,6 +289,10 @@
                         total += jnp.dot(dx[i, q], g[q * n:(q + 1) * n, cols], preferred_element_type=f32)
                     dn_part[i, k] = total.astype(bf16)
 
+            @pl.when(jnp.logical_and(phase == 1, i == 0))
+            def _():
+                down_rest()
+
             ur = i - r
 
             @pl.when(jnp.logical_and(r < R - 1, jnp.logical_and(ur >= 0, ur < units)))
@@ -330,8 +368,10 @@
     def down_drain(phase, units):
         @pl.loop(0, units)
         def _(u):
-            for j in range(1, C):
-                dx_copy(u, lax.rem(c + j, C)).wait_send()
+            for to in far + [sib]:
+                dx_copy(u, to).wait_send()
+            for origin in far:
+                pass_copy(u, origin).wait_send()
             for d in range(R):
                 @pl.when(d > r)
                 def _():
@@ -344,6 +384,17 @@
             @pl.when(phase == 0)
             def _():
                 dy_copy(u).wait_send()
+
+    @pl.when(slab == 0)
+    def _():
+        dx[0, c] = formed(src_t[plan[0, slab, 1]], gain_down[...], jnp.zeros((b, n), bf16))
+        for to in far + [sib]:
+            dx_copy(0, to).start()
+
+    @pl.when(slab == 1)
+    def _():
+        ux[0, r] = formed(src[plan[0, slab, 0]], gain_up[...], jnp.zeros((n, b), bf16))
+        own(0)
 
     @pl.loop(0, 2)
     def _(phase):
@@ -386,11 +437,12 @@
         in_specs=[pl.BlockSpec(memory_space=pltpu.SMEM)] + [vmem] * 5,
         out_specs=(vmem, vmem),
         scratch_shapes=[
-            V(T, R, n, b), V(T, C, n, b), V(T, C, n, b), V(NB, n, b), V(T, n, b), V(NB, n, b),
+            V(T, R, n, b), V(T, C, n, b), V(T, C, n, b), V(T, C, n, b), V(NB, n, b), V(T, n, b), V(NB, n, b),
             V(T, C, b, n), V(T, R, b, n), V(T, R, b, n), V(T, R, b, n), V(T, R, b, n), V(T, R, b, n),
             V(NB, b, n), V(T, b, n), V(NB, b, n),
             D(T, R, 2), D(T, R), D(T, C), D(T, C), D(NB), D(NB),
             D(T, C), D(T, C), D(T, R), D(T, R), D(T, R), D(T, R), D(NB), D(NB),
+            D(T, C), D(T, C), D(T, C),
         ],
         compiler_params=pltpu.CompilerParams(
             collective_id=0, has_side_effects=True, vmem_limit_bytes=56 * 1024 * 1024
@@ -411,7 +463,7 @@
     )
     sizes = mesh.shape
     body = tick_by_tick
-    if sizes["slab"] == 2 and sizes["row"] > 2 and sizes["col"] > 1:
+    if sizes["slab"] == 2 and sizes["row"] > 2 and sizes["col"] % 2 == 0:
         body = functools.partial(two_slabs, sizes["row"], sizes["col"])
     return jax.shard_map(
         body,

time: 146 us -> 144 us (0.986); the launches traced: 143 us -> 144 us
  no operation moved by 1% of the time
where the time goes in v2:
time: 144 us
  Pallas kernels  124 us (86%)
  local copies, waits for them, and re-layouts  19.1 us (13%)
    pallas_call x1, Pallas kernels, two_slabs(): pl.pallas_call(functools.partial(sweep_kernel, R, C, NB, T), out_shape=(j...  124 us
    unnamed x5, local copies, waits for them, and re-layouts  16.9 us

profile of v2, /device:TPU:0, one launch (start us, length us, event | category | flops | bytes accessed | tf_op | source)
XLA Modules:
  0.0 144.1 jit_solution(3227791486334606658)
XLA Ops:
  0.6 1.3 slice_bitcast_fusion
  2.0 1.4 copy.11.plan
  3.3 0.9 copy.13.gain_up
  4.2 2.1 %copy.10 = bf16[1,4,512,128]{2,3,1,0:T(8,128)(2,1)} copy(bf16[1,4,512,128]{3,2,1,0:T(8,128)(2,1)} %param.5) | data formatting | bytes 1048576 | tf_op args[1]
  6.3 10.2 %copy.16 = bf16[256,8,4,512]{3,1,2,0:T(8,128)(2,1)} copy(bf16[256,8,4,512]{3,2,1,0:T(4,128)(2,1)} %bitcast.15) | data formatting | bytes 16777216
  16.5 124.3 %shard_map.59 = (bf16[512,128]{1,0:T(8,128)(2,1)}, bf16[128,512]{1,0:T(8,128)(2,1)}) custom-call(s32[6,2,2]{2,1,0:T(2,128)} %copy.11.plan, bf16[2048,2048]{1,0:T(8,128)(2,1)} %bitcast.16, bf16[4,512,128]{2,1,0:T(8,128)(2,1)} %bitcast.17, bf16[4,128,512]{2,1,0:T(8,128)(2,1)} %bitcast.18, f32[512,1]{1,0:T(8,128)} %copy.13.gain_up, ...), custom_call_target="tpu_custom_call" | custom-call | flops 10737418240 | bytes 8388608 | tf_op jit(solution)/shard_map/pallas_call | solution.py:434
  140.8 1.7 %copy.14 = bf16[1,512,128]{2,1,0:T(8,128)(2,1)} copy(bf16[1,512,128]{1,2,0:T(8,128)(2,1)} %bitcast.20) | data formatting | bytes 262144
  142.5 1.6 %copy.18 = bf16[1,512,128]{2,1,0:T(8,128)(2,1)} copy(bf16[1,512,128]{2,1,0:T(8,128)(2,1)} %bitcast.19) | data formatting | bytes 262144

commit v3 on v2

--- a/solution.py
+++ b/solution.py
@@ -9,6 +9,7 @@
 
 TICKS = 6
 MESH = pl.DeviceIdType.MESH
+CHUNK = 128
 f32 = jnp.float32
 bf16 = jnp.bfloat16
 
@@ -52,19 +53,25 @@
 
 def sweep_kernel(
     R, C, NB, T,
-    plan, g, src, src_t, gain_up, gain_down,
+    plan, raw, src, coupling,
     up_out, down_out,
     ux, up_part, up_got, up_mid, up_first, up_second, up_in,
     dx, dn_part, dn_right, dn_left, dn_from_left, dn_from_right, dn_first, dn_second, dn_in,
     ux_s, ux_r, up_s, up_r, uy_s, uy_r,
     dx_s, dx_r, dr_s, dr_r, dl_s, dl_r, dy_s, dy_r,
     mid_s, mid_r, pass_s,
+    g, src_t, gain_up, gain_down,
 ):
     slab, r, c = lax.axis_index("slab"), lax.axis_index("row"), lax.axis_index("col")
     other = 1 - slab
     n, b = src.shape[1], src.shape[2]
     sib = c + 1 - 2 * lax.rem(c, 2)
     far = [lax.rem(c + j, C) for j in range(2, C, 2)]
+
+    gain_down[...] = coupling[1:2, :]
+    gain_up[...] = jnp.broadcast_to(coupling[0:1, :], (b, n)).T
+    for u in range(NB):
+        src_t[u] = src[u].astype(f32).T.astype(bf16)
 
     barrier = pltpu.get_barrier_semaphore()
     for step in (1, R - 1):
@@ -117,12 +124,6 @@
         return (source.astype(f32) + gain * prev.astype(f32)).astype(bf16)
 
     def up_form(phase, units):
-        @pl.when(phase == 0)
-        def _():
-            @pl.loop(0, NB)
-            def _(u):
-                ux[u, r] = formed(src[u], gain_up[...], jnp.zeros((n, b), bf16))
-
         @pl.when(phase == 1)
         def _():
             @pl.loop(0, NB)
@@ -145,10 +146,6 @@
 
     def up_sweep(phase, units):
         up_form(phase, units)
-
-        @pl.when(phase == 0)
-        def _():
-            own(0)
 
         @pl.loop(0, units + R - 1)
         def _(i):
@@ -247,15 +244,6 @@
             def _():
                 uy_copy(u).wait_send()
 
-    def down_form(phase, units):
-        @pl.when(phase == 0)
-        def _():
-            @pl.loop(0, NB)
-            def _(u):
-                dx[u, c] = formed(src_t[u], gain_down[...], jnp.zeros((b, n), bf16))
-                for to in far + [sib]:
-                    dx_copy(u, to).start()
-
     def down_rest():
         @pl.loop(0, NB)
         def _(u):
@@ -269,8 +257,6 @@
                 dx_copy(t, to).start()
 
     def down_sweep(phase, units):
-        down_form(phase, units)
-
         @pl.loop(0, units + R - 1)
         def _(i):
             @pl.when(i < units)
@@ -396,6 +382,27 @@
         ux[0, r] = formed(src[plan[0, slab, 0]], gain_up[...], jnp.zeros((n, b), bf16))
         own(0)
 
+    @pl.when(slab == 0)
+    def _():
+        @pl.loop(0, NB)
+        def _(u):
+            ux[u, r] = formed(src[u], gain_up[...], jnp.zeros((n, b), bf16))
+
+        own(0)
+
+    @pl.when(slab == 1)
+    def _():
+        @pl.loop(0, NB)
+        def _(u):
+            dx[u, c] = formed(src_t[u], gain_down[...], jnp.zeros((b, n), bf16))
+            for to in far + [sib]:
+                dx_copy(u, to).start()
+
+    @pl.loop(0, raw.shape[0] // CHUNK)
+    def _(q):
+        rows = pl.ds(pl.multiple_of(q * CHUNK, CHUNK), CHUNK)
+        g[rows, :] = raw[rows].reshape(CHUNK, g.shape[1])
+
     @pl.loop(0, 2)
     def _(phase):
         units = jnp.where(phase == 0, NB, T)
@@ -423,18 +430,18 @@
 
 
 def two_slabs(R, C, inverse, sources, coupling, plan):
-    matrix = inverse[0].reshape(inverse.shape[1], -1)
+    raw = inverse[0]
     src = sources[0]
     NB, n, b = src.shape
     T = TICKS
     V = lambda *shape: pltpu.VMEM(shape, bf16)
     D = lambda *shape: pltpu.SemaphoreType.DMA(shape)
     vmem = pl.BlockSpec(memory_space=pltpu.VMEM)
-    flops = 2 * matrix.size * b * (NB + T)
+    flops = 2 * raw.size * b * (NB + T)
     up, down_t = pl.pallas_call(
         functools.partial(sweep_kernel, R, C, NB, T),
         out_shape=(jax.ShapeDtypeStruct((n, b), bf16), jax.ShapeDtypeStruct((b, n), bf16)),
-        in_specs=[pl.BlockSpec(memory_space=pltpu.SMEM)] + [vmem] * 5,
+        in_specs=[pl.BlockSpec(memory_space=pltpu.SMEM)] + [vmem] * 3,
         out_specs=(vmem, vmem),
         scratch_shapes=[
             V(T, R, n, b), V(T, C, n, b), V(T, C, n, b), V(T, C, n, b), V(NB, n, b), V(T, n, b), V(NB, n, b),
@@ -443,13 +450,15 @@
             D(T, R, 2), D(T, R), D(T, C), D(T, C), D(NB), D(NB),
             D(T, C), D(T, C), D(T, R), D(T, R), D(T, R), D(T, R), D(NB), D(NB),
             D(T, C), D(T, C), D(T, C),
+            V(raw.shape[0], raw.shape[1] * raw.shape[2]), V(NB, b, n),
+            pltpu.VMEM((n, b), f32), pltpu.VMEM((1, n), f32),
         ],
         compiler_params=pltpu.CompilerParams(
             collective_id=0, has_side_effects=True, vmem_limit_bytes=56 * 1024 * 1024
         ),
-        cost_estimate=pl.CostEstimate(flops=flops, bytes_accessed=2 * matrix.size, transcendentals=0),
+        cost_estimate=pl.CostEstimate(flops=flops, bytes_accessed=2 * raw.size, transcendentals=0),
     )(
-        plan, matrix, src, jnp.swapaxes(src, 1, 2), coupling[0, 0][:, None], coupling[0, 1][None, :],
+        plan, raw, src, coupling[0],
     )
     return up[None], down_t.T[None]
 

time: 144 us -> 130 us (0.903)
  local copies, waits for them, and re-layouts: 19.1 us -> 4.59 us
    unnamed x5 -> x3, local copies, waits for them, and re-layouts: 16.9 us -> 4.59 us
    another operation x2 -> x0, local copies, waits for them, and re-layouts: 2.22 us -> none  [the longest x1 1.34 us: two_slabs(): coupling[0, 1][None, :]]
where the time goes in v3:
time: 130 us
  Pallas kernels  124 us (95%)
  local copies, waits for them, and re-layouts  4.59 us (4%)
    pallas_call x1, Pallas kernels, two_slabs(): pl.pallas_call(functools.partial(sweep_kernel, R, C, NB, T), out_shape=(j...  124 us
    unnamed x3, local copies, waits for them, and re-layouts  4.59 us

profile of v3, /device:TPU:0, one launch (start us, length us, event | category | flops | bytes accessed | tf_op | source)
XLA Modules:
  0.0 129.5 jit_solution(14763881503278648506)
XLA Ops:
  0.6 1.4 %copy.6.plan = s32[6,2,2]{2,1,0:T(2,128)} copy(s32[6,2,2]{0,2,1:T(2,128)} %param.7) | data formatting | bytes 192 | tf_op args[3]
  2.0 124.3 %shard_map.59 = (bf16[512,128]{1,0:T(8,128)(2,1)}, bf16[128,512]{1,0:T(8,128)(2,1)}) custom-call(s32[6,2,2]{2,1,0:T(2,128)} %copy.6.plan, bf16[2048,4,512]{2,1,0:T(4,128)(2,1)} %bitcast.9, bf16[4,512,128]{2,1,0:T(8,128)(2,1)} %bitcast.10, f32[2,512]{1,0:T(2,128)} %bitcast.11), custom_call_target="tpu_custom_call" | custom-call | flops 10737418240 | bytes 8388608 | tf_op jit(solution)/shard_map/pallas_call | solution.py:441
  126.3 1.7 %copy.7 = bf16[1,512,128]{2,1,0:T(8,128)(2,1)} copy(bf16[1,512,128]{1,2,0:T(8,128)(2,1)} %bitcast.8) | data formatting | bytes 262144
  128.0 1.6 %copy.9 = bf16[1,512,128]{2,1,0:T(8,128)(2,1)} copy(bf16[1,512,128]{2,1,0:T(8,128)(2,1)} %bitcast.7) | data formatting | bytes 262144

commit v4 on v3

--- a/solution.py
+++ b/solution.py
@@ -147,11 +147,15 @@
     def up_sweep(phase, units):
         up_form(phase, units)
 
+        @pl.when(phase == 1)
+        def _():
+            own(1)
+
         @pl.loop(0, units + R - 1)
         def _(i):
-            @pl.when(i + 1 < units)
-            def _():
-                own(i + 1)
+            @pl.when(i + 2 < units)
+            def _():
+                own(i + 2)
 
             for d in reversed(range(1, R)):
                 u = i - (d - 1)
@@ -240,8 +244,7 @@
             for j in range(2, C, 2):
                 mid_copy(u, lax.rem(sib + j, C)).wait_send()
 
-            @pl.when(phase == 0)
-            def _():
+            if phase == 0:
                 uy_copy(u).wait_send()
 
     def down_rest():
@@ -275,10 +278,6 @@
                         total += jnp.dot(dx[i, q], g[q * n:(q + 1) * n, cols], preferred_element_type=f32)
                     dn_part[i, k] = total.astype(bf16)
 
-            @pl.when(jnp.logical_and(phase == 1, i == 0))
-            def _():
-                down_rest()
-
             ur = i - r
 
             @pl.when(jnp.logical_and(r < R - 1, jnp.logical_and(ur >= 0, ur < units)))
@@ -350,6 +349,10 @@
                 @pl.when(jnp.logical_and(r > 0, r < R - 1))
                 def _():
                     finish(mine + dn_from_left[u, r].astype(f32) + dn_from_right[u, r].astype(f32))
+
+            @pl.when(jnp.logical_and(phase == 1, i == 0))
+            def _():
+                down_rest()
 
     def down_drain(phase, units):
         @pl.loop(0, units)
@@ -367,8 +370,7 @@
                 def _():
                     dl_copy(u, d).wait_send()
 
-            @pl.when(phase == 0)
-            def _():
+            if phase == 0:
                 dy_copy(u).wait_send()
 
     @pl.when(slab == 0)
@@ -389,6 +391,7 @@
             ux[u, r] = formed(src[u], gain_up[...], jnp.zeros((n, b), bf16))
 
         own(0)
+        own(1)
 
     @pl.when(slab == 1)
     def _():
@@ -411,20 +414,22 @@
         @pl.when(upward)
         def _():
             up_sweep(phase, units)
-            up_drain(phase, units)
 
         @pl.when(jnp.logical_not(upward))
         def _():
             down_sweep(phase, units)
-            down_drain(phase, units)
 
     @pl.when(slab == 0)
     def _():
+        up_drain(0, NB)
+        down_drain(1, T)
         up_out[...] = up_first[plan[T - 1, slab, 0]]
         down_out[...] = dn_second[T - 1]
 
     @pl.when(slab == 1)
     def _():
+        down_drain(0, NB)
+        up_drain(1, T)
         up_out[...] = up_second[T - 1]
         down_out[...] = dn_first[plan[T - 1, slab, 1]]
 

time: 130 us -> 129 us (level)
  no operation moved by 1% of the time
where the time goes in v4:
time: 129 us
  Pallas kernels  124 us (96%)
  local copies, waits for them, and re-layouts  4.59 us (4%)
    pallas_call x1, Pallas kernels, two_slabs(): pl.pallas_call(functools.partial(sweep_kernel, R, C, NB, T), out_shape=(j...  124 us
    unnamed x3, local copies, waits for them, and re-layouts  4.59 us

profile of v4, /device:TPU:0, one launch (start us, length us, event | category | flops | bytes accessed | tf_op | source)
XLA Modules:
  0.0 128.9 jit_solution(11612578613691101203)
XLA Ops:
  0.6 1.4 %copy.6.plan = s32[6,2,2]{2,1,0:T(2,128)} copy(s32[6,2,2]{0,2,1:T(2,128)} %param.7) | data formatting | bytes 192 | tf_op args[3]
  2.0 123.7 %shard_map.59 = (bf16[512,128]{1,0:T(8,128)(2,1)}, bf16[128,512]{1,0:T(8,128)(2,1)}) custom-call(s32[6,2,2]{2,1,0:T(2,128)} %copy.6.plan, bf16[2048,4,512]{2,1,0:T(4,128)(2,1)} %bitcast.9, bf16[4,512,128]{2,1,0:T(8,128)(2,1)} %bitcast.10, f32[2,512]{1,0:T(2,128)} %bitcast.11), custom_call_target="tpu_custom_call" | custom-call | flops 10737418240 | bytes 8388608 | tf_op jit(solution)/shard_map/pallas_call | solution.py:446
  125.7 1.7 %copy.7 = bf16[1,512,128]{2,1,0:T(8,128)(2,1)} copy(bf16[1,512,128]{1,2,0:T(8,128)(2,1)} %bitcast.8) | data formatting | bytes 262144
  127.4 1.6 %copy.9 = bf16[1,512,128]{2,1,0:T(8,128)(2,1)} copy(bf16[1,512,128]{2,1,0:T(8,128)(2,1)} %bitcast.7) | data formatting | bytes 262144
